TPU v7x, 32 devices: a whole 2x2x4 slice. The times are simulated.
32 devices in a mesh: grp: 2 (over y), gx: 4 (over z), gy: 4 (over x, core).
Axes of the slice: x: 2, y: 2, z: 4, core: 2. Of those that a mesh axis runs over, the one named last changes fastest.
Arguments:
- velocity: bfloat16 [8, 64, 64, 128], P(('grp', 'gx'), None, 'gy'), parts along dimension 0, may hold values from 0.19921875 to 0.41992188
- log_density: bfloat16 [8, 64, 64, 128], P(('grp', 'gx'), None, 'gy'), parts along dimension 0, may hold values from 0 to 0.69921875
- fwd_prev: bfloat16 [8, 256, 64, 128], P(('grp', 'gx'), None, 'gy'), parts along dimension 0, may hold values from -6 to 6
- fwd_now: bfloat16 [8, 256, 64, 128], P(('grp', 'gx'), None, 'gy'), parts along dimension 0, may hold values from -6 to 6
- adj_now: bfloat16 [8, 256, 64, 128], P(('grp', 'gx'), None, 'gy'), parts along dimension 0, may hold values from -6 to 6
- adj_next: bfloat16 [8, 256, 64, 128], P(('grp', 'gx'), None, 'gy'), parts along dimension 0, may hold values from -6 to 6
- wavelet: float32 [8, 3], P(('grp', 'gx')), parts along dimension 0, may hold values from -16 to 16
- source_pos: int32 [8, 3], P(('grp', 'gx')), parts along dimension 0, may hold values from 0 to 127, as said below
- receiver_pos: int32 [8, 3, 256], P(('grp', 'gx')), parts along dimension 0, may hold values from 0 to 127, as said below
- observed: float32 [8, 3, 256], P(('grp', 'gx')), parts along dimension 0, may hold values from -6 to 6
- footprint: int32 [8, 4], P('grp'), parts along dimension 0, may hold values from -1 to 3, as said below
- owner: int32 [4], replicated, may hold values from 0 to 3, each once
Outputs:
- smoothed: float32 [256, 64, 256], P(('grp', 'gx'), 'gy'), parts along dimension 0
There are 2 independent parts, one for each index of `grp`. A program takes and returns all parts, laid end to end along the dimension named above; an argument that names none is the same for every part. Nothing has to cross between parts.
Inputs may be any that keep to these rules, and one draw needn't show every extreme that they name: `footprint`: each row lists blocks start, start + 1, ... in its first two or more slots and -1 after them; some row starts at block 0 and some row ends at block 3, both with all 4 slots live. `source_pos`: source cells lie in the first 128 cells of the window along the first dimension, within the window along the others; some shot's source is at the last such cell in every component and some other shot's at cell 0 in every component. `receiver_pos`: receiver cells lie in the first 128 cells of the window along the first dimension, within the window along the others; some receiver is at the last such cell in every component and some other at cell 0 in every component. `owner`: each index of gx holds exactly one block.
All inputs are finite; a program needn't handle non-finite values.
Results may differ from a plain program's by a relative error of at most 0.0003.
Values may be sent and summed in bfloat16 or wider, within the bound.
A program may use at most 128 MiB of HBM per device.

v0:
```python
import jax
import jax.numpy as jnp
from jax import lax
from jax.sharding import PartitionSpec as P

CX = 64
NZ = 128
NT = 3


SECOND = (-205.0 / 72.0, 8.0 / 5.0, -1.0 / 5.0, 8.0 / 315.0, -1.0 / 560.0)
FIRST = (4.0 / 5.0, -1.0 / 5.0, 4.0 / 105.0, -1.0 / 280.0)


def padded_2(block, sides, width):
    for axis, dim in sides:
        count = lax.axis_size(axis)
        forward = [(i, i + 1) for i in range(count - 1)]
        backward = [(target, source) for source, target in forward]
        low = lax.ppermute(
            lax.slice_in_dim(block, block.shape[dim] - width, None, axis=dim), axis, forward
        )
        high = lax.ppermute(lax.slice_in_dim(block, 0, width, axis=dim), axis, backward)
        block = jnp.concatenate([low, block, high], axis=dim)
    return block


def derivatives(padded, extent):

    def shifted(dimension, offset):
        starts = [4, 4, 4]
        starts[dimension] = 4 + offset
        return padded[
            starts[0] : starts[0] + extent[0],
            starts[1] : starts[1] + extent[1],
            starts[2] : starts[2] + extent[2],
        ]

    laplace = 3.0 * SECOND[0] * shifted(0, 0)
    slopes = []
    for dimension in range(3):
        slope_sum = jnp.zeros(extent, jnp.float32)
        for offset in range(1, 5):
            ahead_cells = shifted(dimension, offset)
            behind = shifted(dimension, -offset)
            laplace = laplace + SECOND[offset] * (ahead_cells + behind)
            slope_sum = slope_sum + FIRST[offset - 1] * (ahead_cells - behind)
        slopes.append(slope_sum)
    return (laplace, slopes)


def operator(padded, extent, squared, density_slopes):
    laplace, slopes = derivatives(padded, extent)
    advect = (
        density_slopes[0] * slopes[0]
        + density_slopes[1] * slopes[1]
        + density_slopes[2] * slopes[2]
    )
    return squared * (laplace - advect)


def kernel_at(depth_value, cells):
    positions = jnp.arange(cells, dtype=jnp.float32)
    distance = jnp.abs(positions[:, None] - positions[None, :])
    length_here = CX * (1.5 + 4.5 * depth_value / (NZ - 1.0))
    weights = jnp.exp(-distance / length_here)
    return weights / jnp.sum(weights, axis=1, keepdims=True)


def pad_sides(field):
    return jnp.pad(field, ((4, 4), (0, 0), (4, 4)))


def on_device(
    velocity,
    log_density,
    fwd_prev,
    fwd_now,
    adj_now,
    adj_next,
    wavelet,
    source_pos,
    receiver_pos,
    observed,
    footprint,
    owner,
):
    shot = lax.axis_index("gx")
    column_index = lax.axis_index("gy")
    block_count = lax.axis_size("gx")
    block_cells, rows_here, depth_cells = (velocity.shape[1], velocity.shape[2], velocity.shape[3])
    slot_count = footprint.shape[1]
    extent = (slot_count * block_cells, rows_here, depth_cells)
    speeds, densities = (
        lax.all_gather(velocity, "gx", axis=0, tiled=True),
        lax.all_gather(log_density, "gx", axis=0, tiled=True),
    )
    blocks = footprint[shot]
    live = blocks >= 0
    holders = owner[jnp.maximum(blocks, 0)]
    livef = live.astype(jnp.float32)[:, None, None, None]
    speed = speeds[holders].astype(jnp.float32)
    squared = (speed * speed * livef).reshape(extent)
    mask = jnp.broadcast_to(livef, speed.shape).reshape(extent)
    density = (densities[holders] * livef.astype(jnp.bfloat16)).reshape(extent)
    density_pad = pad_sides(padded_2(density, (("gy", 1),), 4).astype(jnp.float32))
    unused, density_slopes = derivatives(density_pad, extent)
    x_cells = jnp.arange(extent[0])[:, None, None]
    y_cells = column_index * rows_here + jnp.arange(rows_here)[None, :, None]
    z_cells = jnp.arange(depth_cells)[None, None, :]
    spot = source_pos[0]
    source = ((x_cells == spot[0]) & (y_cells == spot[1]) & (z_cells == spot[2])).astype(
        jnp.float32
    ) * mask
    rec_x = receiver_pos[0, 0]
    rec_local = receiver_pos[0, 1] - column_index * rows_here
    valid = (rec_local >= 0) & (rec_local < rows_here)
    rec_y = jnp.clip(rec_local, 0, rows_here - 1)
    rec_z = receiver_pos[0, 2]

    def apply(field):
        padded = pad_sides(padded_2(field, (("gy", 1),), 4))
        return operator(padded, extent, squared, density_slopes)

    states = [fwd_prev[0].astype(jnp.float32) * mask, fwd_now[0].astype(jnp.float32) * mask]
    residuals = []
    for tick in range(NT):
        older = states[-2]
        current = states[-1]
        newer = 2.0 * current - older + apply(current) + wavelet[0, tick] * source
        states.append(newer)
        residuals.append(newer[rec_x, rec_y, rec_z] - observed[0, tick])
    far_state = adj_next[0].astype(jnp.float32) * mask
    near_state = adj_now[0].astype(jnp.float32) * mask
    image = jnp.zeros(extent, jnp.float32)
    for tick in reversed(range(NT)):
        inject = (
            jnp.zeros(extent, jnp.float32)
            .at[rec_x, rec_y, rec_z]
            .add(jnp.where(valid, residuals[tick], 0.0))
        )
        nearer = 2.0 * near_state - far_state + apply(near_state) + inject * mask
        image = image + nearer * (states[tick + 2] - 2.0 * states[tick + 1] + states[tick])
        far_state = near_state
        near_state = nearer
    received = lax.all_to_all(image, "gx", split_axis=2, concat_axis=0, tiled=True)
    layers = received.shape[2]
    selection = (footprint.reshape(-1)[None, :] == jnp.arange(block_count)[:, None]).astype(
        jnp.float32
    )
    summed = jnp.dot(
        selection,
        received.reshape(footprint.shape[0] * slot_count, -1),
        precision=lax.Precision.HIGHEST,
    )
    field = summed.reshape(block_count * block_cells, rows_here, layers)
    cells_x = field.shape[0]

    def smooth_layer(layer):
        depth_value = (shot * layers + layer).astype(jnp.float32)
        kernel = kernel_at(depth_value, cells_x)
        column = lax.dynamic_index_in_dim(field, layer, 2, keepdims=False)
        return jnp.dot(kernel, column, precision=lax.Precision.HIGHEST).T

    return lax.map(smooth_layer, jnp.arange(layers))


def solution(mesh):
    placed = (
        P(("grp", "gx"), None, "gy", None),
        P(("grp", "gx"), None, "gy", None),
        P(("grp", "gx"), None, "gy", None),
        P(("grp", "gx"), None, "gy", None),
        P(("grp", "gx"), None, "gy", None),
        P(("grp", "gx"), None, "gy", None),
        P(("grp", "gx"), None),
        P(("grp", "gx"), None),
        P(("grp", "gx"), None, None),
        P(("grp", "gx"), None, None),
        P("grp", None),
        P(),
    )
    return jax.shard_map(
        on_device,
        mesh=mesh,
        in_specs=placed,
        out_specs=P(("grp", "gx"), "gy", None),
        check_vma=False,
    )
```

profile of v0, /device:TPU:1, one launch (start us, length us, event | category | flops | bytes accessed | tf_op | source)
XLA Modules:
  0.0 858.2 jit_solution(5600002297495185879)
XLA Ops:
  8.2 1.9 convert_multiply_fusion.3
  10.1 1.4 fusion.104
  11.5 4.5 collective-permute-start.4
  16.0 1.9 collective-permute-start.5
  17.9 1.2 fusion.101
  19.1 3.6 collective-permute-start
  22.8 1.9 collective-permute-start.1
  28.8 6.9 select_maximum_fusion.8
  35.7 3.1 all-gather.5.cloned.1.call-done
  38.8 2.0 gather_fusion.2
  42.3 3.8 collective-permute-start.2
  46.1 1.9 collective-permute-start.3
  48.1 19.8 %all-gather.3.cloned.1.call-done = bf16[4,64,16,128]{3,2,1,0:T(8,128)(2,1)} async-done(((bf16[1,64,16,128]{3,2,1,0:T(8,128)(2,1)}), bf16[4,64,16,128]{3,2,1,0:T(8,128)(2,1)}) %all-gather.3.cloned.1.call-update) | async-done | bytes 1048592 | tf_op jit(solution)/shard_map/all_gather | solution.py:95
  67.9 2.0 gather_fusion.1
  69.9 1.5 convert_multiply_fusion.4
  71.4 1.8 maximum_convert_fusion
  73.2 65.8 %fusion.11 = (f32[256,16,128]{2,1,0:T(8,128)}, f32[256,16,128]{2,1,0:T(8,128)}, f32[256,16,128]{2,1,0:T(8,128)}, f32[256,16,128]{2,1,0:T(8,128)}) fusion(f32[264,24,136]{2,1,0:T(8,128)} %select_maximum_fusion.8, f32[256,4,128]{2,1,0:T(4,128)} %copy-done.11, f32[256,16,128]{2,1,0:T(8,128)} %copy-done.6, f32[256,4,128]{2,1,0:T(4,128)} %copy-done.10, ...), kind=kLoop, calls=%fused_computation.129 | loop fusion | flops 67108864 | bytes 68191744 | tf_op jit(solution)/shard_map/add | solution.py:130
  139.0 1.9 fusion.103
  140.9 3.8 collective-permute-start.6
  144.7 2.1 collective-permute-start.7
  146.9 3.9 collective-permute-done.6
  150.8 4.4 collective-permute-done.7
  155.2 6.9 select_maximum_fusion.6
  162.1 60.9 %fusion.12 = f32[256,16,128]{2,1,0:T(8,128)} fusion(f32[256,16,128]{2,1,0:T(8,128)} %get-tuple-element.108, f32[256,16,128]{2,1,0:T(8,128)} %get-tuple-element.107, f32[256,16,128]{2,1,0:T(8,128)} %get-tuple-element.106, f32[264,24,136]{2,1,0:T(8,128)} %select_maximum_fusion.6, f32[256,4,128]{2,1,0:T(4,128)} %copy-done.13, ...), kind=kLoop, calls=%fused_computation.130 | loop fusion | flops 49807360 | bytes 48239748 | tf_op jit(solution)/shard_map/add | solution.py:130
  223.0 2.8 fusion.102
  225.9 1.9 collective-permute-start.8
  227.8 3.6 collective-permute-start.9
  231.4 8.7 %select_maximum_fusion.10 = f32[264,24,136]{2,1,0:T(8,128)} fusion(f32[256,4,128]{2,1,0:T(4,128)} %collective-permute-done.1, f32[256,16,128]{2,1,0:T(8,128)S(1)} %copy-done.5, f32[256,4,128]{2,1,0:T(4,128)} %collective-permute-done), kind=kLoop, calls=%fused_computation.49 | loop fusion | flops 12925440 | bytes 6592512 | tf_op jit(solution)/shard_map/concatenate | solution.py:24
  240.1 3.6 gather_fusion.5
  243.8 3.6 gather_fusion.4
  247.4 9.0 %select_maximum_fusion.4 = f32[264,24,136]{2,1,0:T(8,128)} fusion(f32[256,4,128]{2,1,0:T(4,128)} %collective-permute-done.9, f32[256,16,128]{2,1,0:T(8,128)} %fusion.12, f32[256,4,128]{2,1,0:T(4,128)} %collective-permute-done.8), kind=kLoop, calls=%fused_computation.43 | loop fusion | flops 12925440 | bytes 6592512 | tf_op jit(solution)/shard_map/concatenate | solution.py:24
  256.5 64.6 %fusion.13 = f32[256,16,128]{2,1,0:T(8,128)} fusion(f32[256,16,128]{2,1,0:T(8,128)} %get-tuple-element.108, f32[256,16,128]{2,1,0:T(8,128)} %get-tuple-element.107, f32[256,16,128]{2,1,0:T(8,128)} %get-tuple-element.106, f32[264,24,136]{2,1,0:T(8,128)} %select_maximum_fusion.4, f32[256,4,128]{2,1,0:T(4,128)} %collective-permute-done.9, ...), kind=kLoop, calls=%fused_computation.131 | loop fusion | flops 48758784 | bytes 49288324 | tf_op jit(solution)/shard_map/add | solution.py:130
  321.1 3.6 gather_fusion.3
  324.7 1.5 broadcast.238.clone.2
  326.2 33.7 %scatter_fusion = f32[256,16,128]{2,1,0:T(8,128)} fusion(f32[256,16,128]{2,1,0:T(8,128)} %broadcast.238.clone.2, s32[256]{0:T(256)S(1)} %bitcast.96, f32[256]{0:T(256)S(1)} %get-tuple-element.130), kind=kCustom, calls=%fused_computation.6 | custom fusion | flops 256 | bytes 6144 | tf_op jit(solution)/shard_map/scatter-add | solution.py:140
  359.9 60.5 %fusion.86 = f32[256,16,128]{2,1,0:T(8,128)} fusion(f32[256,16,128]{2,1,0:T(8,128)} %scatter_fusion, f32[256,16,128]{2,1,0:T(8,128)} %get-tuple-element.108, f32[256,16,128]{2,1,0:T(8,128)} %get-tuple-element.107, f32[256,16,128]{2,1,0:T(8,128)} %get-tuple-element.106, f32[264,24,136]{2,1,0:T(8,128)} %select_maximum_fusion.10, ...), kind=kLoop, calls=%fused_computation.223 | loop fusion | flops 48758784 | bytes 50332672 | tf_op jit(solution)/shard_map/add | solution.py:142
  420.4 2.7 fusion.100
  423.1 2.2 collective-permute-start.10
  425.3 2.9 collective-permute-start.11
  428.2 1.5 broadcast.238.clone.1
  429.6 33.5 %scatter_fusion.1 = f32[256,16,128]{2,1,0:T(8,128)} fusion(f32[256,16,128]{2,1,0:T(8,128)} %broadcast.238.clone.1, s32[256]{0:T(256)S(1)} %bitcast.97, f32[256]{0:T(256)S(1)} %get-tuple-element.132), kind=kCustom, calls=%fused_computation.7 | custom fusion | flops 256 | bytes 6144 | tf_op jit(solution)/shard_map/scatter-add | solution.py:140
  463.1 9.0 %select_maximum_fusion.2 = f32[264,24,136]{2,1,0:T(8,128)} fusion(f32[256,4,128]{2,1,0:T(4,128)} %collective-permute-done.11, f32[256,16,128]{2,1,0:T(8,128)} %fusion.86, f32[256,4,128]{2,1,0:T(4,128)} %collective-permute-done.10), kind=kLoop, calls=%fused_computation.41 | loop fusion | flops 12925440 | bytes 6592512 | tf_op jit(solution)/shard_map/concatenate | solution.py:24
  472.1 59.9 %multiply_add_fusion = f32[256,16,128]{2,1,0:T(8,128)} fusion(f32[256,16,128]{2,1,0:T(8,128)} %scatter_fusion.1, f32[256,16,128]{2,1,0:T(8,128)} %get-tuple-element.108, f32[256,16,128]{2,1,0:T(8,128)} %get-tuple-element.107, f32[256,16,128]{2,1,0:T(8,128)} %get-tuple-element.106, f32[264,24,136]{2,1,0:T(8,128)} %select_maximum_fusion.2, ...), kind=kLoop, calls=%fused_computation.226 | loop fusion | flops 48758784 | bytes 50332672 | tf_op jit(solution)/shard_map/add | solution.py:142
  532.1 2.7 fusion.99
  534.8 2.6 collective-permute-start.12
  537.4 2.5 collective-permute-start.13
  539.9 1.5 broadcast.238.clone
  541.3 33.7 %scatter_fusion.2 = f32[256,16,128]{2,1,0:T(8,128)} fusion(f32[256,16,128]{2,1,0:T(8,128)} %broadcast.238.clone, s32[256]{0:T(256)S(1)} %bitcast.98, f32[256]{0:T(256)S(1)} %get-tuple-element.131), kind=kCustom, calls=%fused_computation.8 | custom fusion | flops 256 | bytes 6144 | tf_op jit(solution)/shard_map/scatter-add | solution.py:140
  575.0 9.0 %select_maximum_fusion = f32[264,24,136]{2,1,0:T(8,128)} fusion(f32[256,4,128]{2,1,0:T(4,128)} %collective-permute-done.13, f32[256,16,128]{2,1,0:T(8,128)} %multiply_add_fusion, f32[256,4,128]{2,1,0:T(4,128)} %collective-permute-done.12), kind=kLoop, calls=%fused_computation.39 | loop fusion | flops 12925440 | bytes 6592512 | tf_op jit(solution)/shard_map/concatenate | solution.py:24
  584.0 63.9 %fusion.83 = f32[256,16,128]{2,1,0:T(8,128)} fusion(f32[256,16,128]{2,1,0:T(8,128)} %get-tuple-element.105, f32[256,16,128]{2,1,0:T(8,128)} %scatter_fusion.2, f32[256,16,128]{2,1,0:T(8,128)} %get-tuple-element.108, f32[256,16,128]{2,1,0:T(8,128)} %get-tuple-element.107, f32[256,16,128]{2,1,0:T(8,128)} %get-tuple-element.106, ...), kind=kLoop, calls=%fused_computation.218 | loop fusion | flops 57147392 | bytes 59769856 | tf_op jit(solution)/shard_map/add | solution.py:143
  647.9 3.2 copy.24
  651.1 3.9 all-to-all-start
  655.1 48.5 %all-to-all-done = f32[256,16,128]{0,1,2:T(8,128)S(1)} async-done(((f32[256,16,128]{0,1,2:T(8,128)}), f32[256,16,128]{0,1,2:T(8,128)S(1)}, u32[]{:S(2)}, u32[]{:S(2)}) %all-to-all-start) | async-done | bytes 2097184 | tf_op jit(solution)/shard_map/all_to_all | solution.py:146
  703.6 6.6 copy.26
  710.2 6.0 reshape.212
  717.7 1.3 copy.27
  719.0 131.2 %while.12 = (s32[]{:T(128)}, f32[32,16,256]{2,1,0:T(8,128)}, s32[32]{0:T(128)S(1)}, f32[256,16,32]{0,1,2:T(8,128)S(1)}, s32[]{:T(128)}, /*index=5*/s32[]{:T(128)...) while((s32[]{:T(128)}, f32[32,16,256]{2,1,0:T(8,128)}, s32[32]{0:T(128)S(1)}, ...), condition=%wide.region_5.6_spmd, body=%wide.region_3.5_spmd.sunk | while | flops 13238026 | bytes 35551 | solution.py:165
  722.1 1.0 fusion.117
  726.2 1.0 fusion.117
  730.3 1.0 fusion.117
  734.4 1.0 fusion.117
  738.5 1.0 fusion.117
  742.6 1.0 fusion.117
  746.7 1.0 fusion.117
  (170 shorter events, 59.5 us)
Async XLA Ops:
  6.5 18.2 %copy-start = (s32[4]{0:T(128)S(1)}, s32[4]{0:T(128)}, u32[]{:S(2)}) copy-start(s32[4]{0:T(128)} %param.25) | copy-start | bytes 52
  6.5 32.3 %all-gather.5.cloned.1.call-start = ((), (), s32[]{:S(2)}) async-start(), calls=%async_computation.2 | async-start | bytes 1310720 | tf_op jit(solution)/shard_map/all_gather | solution.py:96
  7.3 60.6 %all-gather.3.cloned.1.call-start = ((), (), s32[]{:S(2)}) async-start(), calls=%async_computation.1 | async-start | bytes 1310720 | tf_op jit(solution)/shard_map/all_gather | solution.py:95
  10.1 9.1 %copy-start.4 = (f32[256,16,128]{2,1,0:T(8,128)}, f32[256,16,128]{2,1,0:T(8,128)S(1)}, u32[]{:S(2)}) copy-start(f32[256,16,128]{2,1,0:T(8,128)S(1)} %get-tuple-element.128) | copy-start | bytes 6291460
  10.1 18.7 %copy-start.6 = (f32[256,16,128]{2,1,0:T(8,128)}, f32[256,16,128]{2,1,0:T(8,128)S(1)}, u32[]{:S(2)}) copy-start(f32[256,16,128]{2,1,0:T(8,128)S(1)} %get-tuple-element.129) | copy-start | bytes 6291460
  10.1 14.7 %copy-start.17 = (s32[4,4]{1,0:T(4,128)S(1)}, s32[4,4]{1,0:T(4,128)}, u32[]{:S(2)}) copy-start(s32[4,4]{1,0:T(4,128)} %param.24) | copy-start | bytes 196
  10.1 15.5 %copy-start.15 = (s32[1,3]{1,0:T(1,128)S(1)}, s32[1,3]{1,0:T(1,128)}, u32[]{:S(2)}) copy-start(s32[1,3]{1,0:T(1,128)} %param.21) | copy-start | bytes 40
  10.1 17.4 %copy-start.16 = (f32[1,3]{1,0:T(1,128)S(1)}, f32[1,3]{1,0:T(1,128)}, u32[]{:S(2)}) copy-start(f32[1,3]{1,0:T(1,128)} %param.20) | copy-start | bytes 40
  11.5 17.3 %collective-permute-start.4 = (f32[256,4,128]{2,1,0:T(4,128)}, f32[256,4,128]{2,1,0:T(4,128)S(1)}, u32[]{:S(2)}, u32[]{:S(2)}) collective-permute-start(f32[256,4,128]{2,1,0:T(4,128)} %get-tuple-element.121), channel_id=1, source_target_pairs={{0,1},{1,2},{2,3},{4,5},{5,6},{6,7},{8,9},{9,10},{10,11},{12,13},{... | collective-permute-start | bytes 1572872 | tf_op jit(solution)/shard_map/ppermute | solution.py:20
  16.0 12.8 %collective-permute-start.5 = (f32[256,4,128]{2,1,0:T(4,128)}, f32[256,4,128]{2,1,0:T(4,128)S(1)}, u32[]{:S(2)}, u32[]{:S(2)}) collective-permute-start(f32[256,4,128]{2,1,0:T(4,128)} %get-tuple-element.122), channel_id=1, source_target_pairs={{1,0},{2,1},{3,2},{5,4},{6,5},{7,6},{9,8},{10,9},{11,10},{13,12},{... | collective-permute-start | bytes 1572872 | tf_op jit(solution)/shard_map/ppermute | solution.py:23
  19.1 212.3 %collective-permute-start = (f32[256,4,128]{2,1,0:T(4,128)}, f32[256,4,128]{2,1,0:T(4,128)}, u32[]{:S(2)}, u32[]{:S(2)}) collective-permute-start(f32[256,4,128]{2,1,0:T(4,128)} %get-tuple-element.115), channel_id=1, source_target_pairs={{0,1},{1,2},{2,3},{4,5},{5,6},{6,7},{8,9},{9,10},{10,11},{12,13},{... | collective-permute-start | bytes 1572872 | tf_op jit(solution)/shard_map/ppermute | solution.py:20
  22.8 208.7 %collective-permute-start.1 = (f32[256,4,128]{2,1,0:T(4,128)}, f32[256,4,128]{2,1,0:T(4,128)}, u32[]{:S(2)}, u32[]{:S(2)}) collective-permute-start(f32[256,4,128]{2,1,0:T(4,128)} %get-tuple-element.116), channel_id=1, source_target_pairs={{1,0},{2,1},{3,2},{5,4},{6,5},{7,6},{9,8},{10,9},{11,10},{13,12},{... | collective-permute-start | bytes 1572872 | tf_op jit(solution)/shard_map/ppermute | solution.py:23
  28.8 6.9 copy-start.10
  28.8 6.9 copy-start.11
  41.2 1.0 copy-start.8
  42.3 29.0 %collective-permute-start.2 = (bf16[256,4,128]{2,1,0:T(4,128)(2,1)S(1)}, bf16[256,4,128]{2,1,0:T(4,128)(2,1)S(1)}, u32[]{:S(2)}, u32[]{:S(2)}) collective-permute-start(bf16[256,4,128]{2,1,0:T(4,128)(2,1)S(1)} %get-tuple-element.123), channel_id=1, source_target_pairs={{0,1},{1,2},{2,3},{4,5},{5,6},{6,7},{8,9},{9,10},{10,11},{12,13},{... | collective-permute-start | bytes 786440 | tf_op jit(solution)/shard_map/ppermute | solution.py:20
  46.1 25.2 %collective-permute-start.3 = (bf16[256,4,128]{2,1,0:T(4,128)(2,1)S(1)}, bf16[256,4,128]{2,1,0:T(4,128)(2,1)}, u32[]{:S(2)}, u32[]{:S(2)}) collective-permute-start(bf16[256,4,128]{2,1,0:T(4,128)(2,1)S(1)} %get-tuple-element.124), channel_id=1, source_target_pairs={{1,0},{2,1},{3,2},{5,4},{6,5},{7,6},{9,8},{10,9},{11,10},{13,12},{... | collective-permute-start | bytes 786440 | tf_op jit(solution)/shard_map/ppermute | solution.py:23
  69.8 1.5 copy-start.9
  139.0 7.9 copy-start.14
  139.0 7.9 copy-start.18
  139.0 16.2 %copy-start.3 = (f32[256,16,128]{2,1,0:T(8,128)S(1)}, f32[256,16,128]{2,1,0:T(8,128)}, u32[]{:S(2)}) copy-start(f32[256,16,128]{2,1,0:T(8,128)} %get-tuple-element.105) | copy-start | bytes 6291460
  140.9 9.9 %collective-permute-start.6 = (f32[256,4,128]{2,1,0:T(4,128)S(1)}, f32[256,4,128]{2,1,0:T(4,128)S(1)}, u32[]{:S(2)}, u32[]{:S(2)}) collective-permute-start(f32[256,4,128]{2,1,0:T(4,128)S(1)} %get-tuple-element.119), channel_id=1, source_target_pairs={{0,1},{1,2},{2,3},{4,5},{5,6},{6,7},{8,9},{9,10},{10,11},{12,13},{... | collective-permute-start | bytes 1572872 | tf_op jit(solution)/shard_map/ppermute | solution.py:20
  144.7 10.5 %collective-permute-start.7 = (f32[256,4,128]{2,1,0:T(4,128)S(1)}, f32[256,4,128]{2,1,0:T(4,128)S(1)}, u32[]{:S(2)}, u32[]{:S(2)}) collective-permute-start(f32[256,4,128]{2,1,0:T(4,128)S(1)} %get-tuple-element.120), channel_id=1, source_target_pairs={{1,0},{2,1},{3,2},{5,4},{6,5},{7,6},{9,8},{10,9},{11,10},{13,12},{... | collective-permute-start | bytes 1572872 | tf_op jit(solution)/shard_map/ppermute | solution.py:23
  146.9 15.2 %copy-start.2 = (f32[4,64,16,128]{3,2,1,0:T(8,128)S(1)}, f32[4,64,16,128]{3,2,1,0:T(8,128)}, u32[]{:S(2)}) copy-start(f32[4,64,16,128]{3,2,1,0:T(8,128)} %convert_multiply_fusion.4) | copy-start | bytes 6291460
  146.9 15.2 %copy-start.7 = (bf16[1,256,16,128]{3,2,1,0:T(8,128)(2,1)S(1)}, bf16[1,256,16,128]{3,2,1,0:T(8,128)(2,1)}, u32[]{:S(2)}) copy-start(bf16[1,256,16,128]{3,2,1,0:T(8,128)(2,1)} %param.17) | copy-start | bytes 3145732
  150.8 11.3 %copy-start.12 = (f32[256,4,128]{2,1,0:T(4,128)}, f32[256,4,128]{2,1,0:T(4,128)S(1)}, u32[]{:S(2)}) copy-start(f32[256,4,128]{2,1,0:T(4,128)S(1)} %collective-permute-done.6) | copy-start | bytes 1572868
  155.2 6.9 copy-start.13
  223.0 8.4 copy-start.5
  225.9 21.5 %collective-permute-start.8 = (f32[256,4,128]{2,1,0:T(4,128)}, f32[256,4,128]{2,1,0:T(4,128)}, u32[]{:S(2)}, u32[]{:S(2)}) collective-permute-start(f32[256,4,128]{2,1,0:T(4,128)} %get-tuple-element.117), channel_id=1, source_target_pairs={{0,1},{1,2},{2,3},{4,5},{5,6},{6,7},{8,9},{9,10},{10,11},{12,13},{... | collective-permute-start | bytes 1572872 | tf_op jit(solution)/shard_map/ppermute | solution.py:20
  227.8 19.6 %collective-permute-start.9 = (f32[256,4,128]{2,1,0:T(4,128)}, f32[256,4,128]{2,1,0:T(4,128)}, u32[]{:S(2)}, u32[]{:S(2)}) collective-permute-start(f32[256,4,128]{2,1,0:T(4,128)} %get-tuple-element.118), channel_id=1, source_target_pairs={{1,0},{2,1},{3,2},{5,4},{6,5},{7,6},{9,8},{10,9},{11,10},{13,12},{... | collective-permute-start | bytes 1572872 | tf_op jit(solution)/shard_map/ppermute | solution.py:23
  423.1 40.1 %collective-permute-start.10 = (f32[256,4,128]{2,1,0:T(4,128)}, f32[256,4,128]{2,1,0:T(4,128)}, u32[]{:S(2)}, u32[]{:S(2)}) collective-permute-start(f32[256,4,128]{2,1,0:T(4,128)} %get-tuple-element.113), channel_id=1, source_target_pairs={{0,1},{1,2},{2,3},{4,5},{5,6},{6,7},{8,9},{9,10},{10,11},{12,13},{... | collective-permute-start | bytes 1572872 | tf_op jit(solution)/shard_map/ppermute | solution.py:20
  425.3 37.8 %collective-permute-start.11 = (f32[256,4,128]{2,1,0:T(4,128)}, f32[256,4,128]{2,1,0:T(4,128)}, u32[]{:S(2)}, u32[]{:S(2)}) collective-permute-start(f32[256,4,128]{2,1,0:T(4,128)} %get-tuple-element.114), channel_id=1, source_target_pairs={{1,0},{2,1},{3,2},{5,4},{6,5},{7,6},{9,8},{10,9},{11,10},{13,12},{... | collective-permute-start | bytes 1572872 | tf_op jit(solution)/shard_map/ppermute | solution.py:23
  534.8 40.3 %collective-permute-start.12 = (f32[256,4,128]{2,1,0:T(4,128)}, f32[256,4,128]{2,1,0:T(4,128)}, u32[]{:S(2)}, u32[]{:S(2)}) collective-permute-start(f32[256,4,128]{2,1,0:T(4,128)} %get-tuple-element.111), channel_id=1, source_target_pairs={{0,1},{1,2},{2,3},{4,5},{5,6},{6,7},{8,9},{9,10},{10,11},{12,13},{... | collective-permute-start | bytes 1572872 | tf_op jit(solution)/shard_map/ppermute | solution.py:20
  537.4 37.6 %collective-permute-start.13 = (f32[256,4,128]{2,1,0:T(4,128)}, f32[256,4,128]{2,1,0:T(4,128)}, u32[]{:S(2)}, u32[]{:S(2)}) collective-permute-start(f32[256,4,128]{2,1,0:T(4,128)} %get-tuple-element.112), channel_id=1, source_target_pairs={{1,0},{2,1},{3,2},{5,4},{6,5},{7,6},{9,8},{10,9},{11,10},{13,12},{... | collective-permute-start | bytes 1572872 | tf_op jit(solution)/shard_map/ppermute | solution.py:23
  651.1 52.5 %all-to-all-start = ((f32[256,16,128]{0,1,2:T(8,128)}), f32[256,16,128]{0,1,2:T(8,128)S(1)}, u32[]{:S(2)}, u32[]{:S(2)}) async-start(f32[256,16,128]{0,1,2:T(8,128)} %copy.24), calls=%async_computation | async-start | bytes 4194304 | tf_op jit(solution)/shard_map/all_to_all | solution.py:146
  850.2 0.7 copy-start.1
Sparse Core Ops, SparseCore 0:
  8.9 29.8 all-gather.4
  40.4 27.4 all-gather.2
where the time goes:
time: 870 us; the launch traced here: 858 us
  other arithmetic  540 us (62%)
  waiting for transfers between devices  80.4 us (9%)
  loops' own time  74.1 us (9%)
  local copies, waits for them, and re-layouts  72.7 us (8%)
  starting transfers between devices  43.3 us (5%)
  matrix products  33.3 us (4%)
  between operations  14.4 us (2%)
    add x3, other arithmetic, on_device(): newer = 2.0 * current - older + apply(current) + wavelet[0, tick] * source  191 us
    add x2, other arithmetic, on_device(): nearer = 2.0 * near_state - far_state + apply(near_state) + inject * mask  120 us
    scatter-add x3, other arithmetic, on_device(): inject = jnp.zeros(extent, jnp.float32).at[rec_x, rec_y, rec_z].add(jnp.w...  101 us
    another operation x1, loops' own time, on_device(): return lax.map(smooth_layer, jnp.arange(layers))  74.1 us
    add x1, other arithmetic, on_device(): image + nearer * (states[tick + 2] - 2.0 * states[tick + 1] + states[tick])  63.9 us
    concatenate x6, other arithmetic, padded_2(): block = jnp.concatenate([low, block, high], axis=dim)  49.4 us
    all_to_all x1, waiting for transfers between devices, on_device(): lax.all_to_all(image, 'gx', split_axis=2, concat_axis=0, tiled=True)  48.5 us
    dot_general x32, matrix products, smooth_layer(): return jnp.dot(kernel, column, precision=lax.Precision.HIGHEST).T  32.6 us
  transfers between devices with their start and end apart: 17, of which 5 were waited for; matrix products, arithmetic and copies ran while one was open for 29% of the time, Pallas kernels for 0%

commit v1 on v0

v1 whole, which is shorter than its diff:
```python
import functools

import jax
import jax.numpy as jnp
import numpy as np
from jax import lax
from jax.experimental import pallas as pl
from jax.experimental.pallas import tpu as pltpu
from jax.sharding import PartitionSpec as P

CX = 64
NZ = 128
NT = 3
H = 4
SECOND = (-14350.0, 8064.0, -1008.0, 128.0, -9.0)
FIRST = (672.0, -168.0, 32.0, -3.0)
BF = jnp.bfloat16
F32 = jnp.float32
CHUNK = 32


def band(size):
    first = np.zeros((size, size), np.float32)
    second = np.zeros((size, size), np.float32)
    for k in range(1, 5):
        ahead = np.eye(size, k=k, dtype=np.float32)
        first += FIRST[k - 1] * (ahead - ahead.T)
        second += SECOND[k] * (ahead + ahead.T)
    return first, second


def dot(a, b):
    return jnp.dot(a, b, preferred_element_type=F32)


def split(u):
    hi = u.astype(BF)
    return hi, (u - hi.astype(F32)).astype(BF)


def wave_kernel(
    dims,
    scal, fprev, fnow, anow, anext, speed, dens, maskp, code_col, code_row, recz, obs, dx, mz,
    out,
    p0, p1, p2, q3, q2, q1, acc, sq, grad, den, xt, xo, hot, vsum, inj,
    send_sem, recv_sem,
):
    rows, span, depth = dims
    half = span // 2
    gy = lax.axis_index("gy")
    count = lax.axis_size("gy")
    has_left = gy > 0
    has_right = gy < count - 1
    barrier = pltpu.get_barrier_semaphore()
    steps = (den, p0, q3, p1, p2, q2, q1)

    @pl.when(has_left)
    def _():
        pl.semaphore_signal(barrier, inc=1, device_id={"gy": gy - 1}, device_id_type=pl.DeviceIdType.MESH)

    @pl.when(has_right)
    def _():
        pl.semaphore_signal(barrier, inc=1, device_id={"gy": gy + 1}, device_id_type=pl.DeviceIdType.MESH)

    @pl.when(jnp.logical_not(has_left))
    def _():
        for buf in steps:
            buf[0:H] = jnp.zeros((H, span, depth), buf.dtype)

    @pl.when(jnp.logical_not(has_right))
    def _():
        for buf in steps:
            buf[rows + H : rows + 2 * H] = jnp.zeros((H, span, depth), buf.dtype)

    pl.semaphore_wait(barrier, has_left.astype(jnp.int32) + has_right.astype(jnp.int32))

    def to_left(e):
        buf = steps[e]
        return pltpu.make_async_remote_copy(
            src_ref=buf.at[pl.ds(H, H)], dst_ref=buf.at[pl.ds(rows + H, H)],
            send_sem=send_sem.at[e, 0], recv_sem=recv_sem.at[e, 0],
            device_id={"gy": gy - 1}, device_id_type=pl.DeviceIdType.MESH)

    def to_right(e):
        buf = steps[e]
        return pltpu.make_async_remote_copy(
            src_ref=buf.at[pl.ds(rows, H)], dst_ref=buf.at[pl.ds(0, H)],
            send_sem=send_sem.at[e, 1], recv_sem=recv_sem.at[e, 1],
            device_id={"gy": gy + 1}, device_id_type=pl.DeviceIdType.MESH)

    def send(e):
        @pl.when(has_left)
        def _():
            to_left(e).start()

        @pl.when(has_right)
        def _():
            to_right(e).start()

    def receive(e):
        @pl.when(has_right)
        def _():
            to_left(e).wait_recv()

        @pl.when(has_left)
        def _():
            to_right(e).wait_recv()

    def turn(src, put):
        acc[0] = src[...].astype(F32)

        @pl.loop(0, rows)
        def _(y):
            put(y, acc[0, pl.ds(y, span, stride=rows), :])

    mask = maskp[...]

    def into(buf):
        def put(y, u):
            buf[y + H] = (u * mask).astype(buf.dtype)
        return put

    def put_speed(y, u):
        sq[y] = u * u * mask * (1.0 / 5040.0)

    turn(dens, into(den))
    send(0)
    turn(fnow, into(p0))
    send(1)
    turn(anow, into(q3))
    send(2)
    turn(fprev, into(p1))
    turn(anext, into(q2))
    turn(speed, put_speed)

    source_x, source_y, source_z = scal[0], scal[1], scal[2]
    at_x = lax.broadcasted_iota(jnp.int32, (span, depth), 0).astype(F32) == source_x
    at_z = lax.broadcasted_iota(jnp.int32, (span, depth), 1).astype(F32) == source_z
    hot[...] = jnp.where(at_x & at_z, mask, 0.0)
    nrec = recz.shape[0]
    mask2 = jnp.concatenate([mask[:half]] * (nrec // depth), axis=1)

    @pl.loop(0, rows)
    def _(y):
        lanes = lax.broadcasted_iota(jnp.int32, (nrec, half), 1) + y * half
        xt[y] = jnp.where(lanes == code_col[...], 1.0, 0.0).astype(BF)
        subs = lax.broadcasted_iota(jnp.int32, (half, nrec), 0) + y * half
        xo[y] = jnp.where(subs == code_row[...], mask2, 0.0).astype(BF)

    def planes(first, receive_from, body):
        @pl.loop(H, rows - H)
        def _(y):
            body(y)

        receive(receive_from)

        @pl.loop(0, 2 * H)
        def _(k):
            body(k + (rows - 2 * H) * (k // H))

    def slope(y):
        u = den[y + H]
        grad[0, y] = dot(dx[0:span, :], u) * (6.0 / 840.0)
        grad[2, y] = dot(u, mz[0:depth, 0:depth]) * (6.0 / 840.0)
        total = jnp.zeros((span, depth), F32)
        for k in range(1, 5):
            total = total + FIRST[k - 1] * (den[y + H + k].astype(F32) - den[y + H - k].astype(F32))
        grad[1, y] = total * (6.0 / 840.0)

    planes(0, 0, slope)

    def spatial(buf, y, exact, finish):
        u = buf[y + H]
        if exact:
            hi = u.astype(BF)
            along_z = dot(hi, mz[0:depth, :])
            along_x = dot(dx[...], hi)
        else:
            both = jnp.concatenate(split(u), axis=1)
            along_z = dot(both, mz[...])
            along_x = dot(dx[...], both)
        for r in range(0, span, CHUNK):
            rs = slice(r, r + CHUNK)
            first_x = along_x[rs, 0:depth]
            second_x = along_x[span + r : span + r + CHUNK, 0:depth]
            if not exact:
                first_x = first_x + along_x[rs, depth:]
                second_x = second_x + along_x[span + r : span + r + CHUNK, depth:]
            center = buf[y + H, rs, :]
            lap = (3.0 * SECOND[0]) * center + second_x + along_z[rs, depth:]
            slope_y = None
            for k in range(1, 5):
                up = buf[y + H + k, rs, :]
                down = buf[y + H - k, rs, :]
                lap = lap + SECOND[k] * (up + down)
                term = FIRST[k - 1] * (up - down)
                slope_y = term if slope_y is None else slope_y + term
            adv = (
                grad[0, y, rs, :] * first_x
                + grad[1, y, rs, :] * slope_y
                + grad[2, y, rs, :] * along_z[rs, 0:depth]
            )
            finish(r, rs, center, sq[y, rs, :] * (lap - adv))

    def acc_rows(t, y, r):
        return acc.at[t, pl.ds(pl.multiple_of(y * span + r, CHUNK), CHUNK), :]

    pressures = (p0, p1, p2)
    for t in range(NT):
        cur = pressures[t]
        vsum[...] = jnp.zeros_like(vsum)

        def forward(y, t=t, cur=cur):
            amount = jnp.where(y.astype(F32) == source_y, scal[3 + t], 0.0)
            pieces = []

            def finish(r, rs, center, lu):
                value = lu + amount * hot[rs, :]
                acc_rows(t, y, r)[...] = value
                old = p1[y + H, rs, :] if t == 0 else pressures[t - 1][y + H, rs, :]
                new = 2.0 * center - old + value
                if t < NT - 1:
                    pressures[t + 1][y + H, rs, :] = new
                if r < half:
                    pieces.append(new)

            spatial(cur, y, t == 0, finish)
            read = dot(xt[y], jnp.concatenate(split(jnp.concatenate(pieces, axis=0)), axis=1))
            vsum[...] += read[:, 0:depth] + read[:, depth:]

        planes(0, (1, 3, 4)[t], forward)
        if t < NT - 1:
            send(3 + t)
        here = lax.broadcasted_iota(jnp.int32, (nrec, depth), 1) == recz[...]
        residual = jnp.where(here, vsum[...] - obs[t], 0.0)
        hi, lo = split(residual)
        inj[t, :, 0:depth] = hi
        inj[t, :, depth:] = lo

    adjoint = {3: q3, 2: q2, 1: q1}
    for t in reversed(range(NT)):
        cur = adjoint[t + 1]

        def backward(y, t=t, cur=cur):
            added = dot(xo[y], inj[t])
            added = added[:, 0:depth] + added[:, depth:]
            images = []

            def finish(r, rs, center, lu):
                old = q2[y + H, rs, :] if t == NT - 1 else adjoint[t + 2][y + H, rs, :]
                new = 2.0 * center - old + lu
                if r < half:
                    new = new + added[rs]
                if t > 0:
                    adjoint[t][y + H, rs, :] = new
                term = new * acc_rows(t, y, r)[...]
                if t < NT - 1:
                    term = term + acc_rows(t + 1, y, r)[...]
                if t > 0:
                    acc_rows(t, y, r)[...] = term
                else:
                    images.append(term)

            spatial(cur, y, t == NT - 1, finish)
            if t == 0:
                out[y] = jnp.concatenate(images, axis=0).T

        planes(0, (6, 5, 2)[t], backward)
        if t > 0:
            send(5 + NT - 1 - t)

    for e in range(7):
        @pl.when(has_left)
        def _():
            to_left(e).wait_send()

        @pl.when(has_right)
        def _():
            to_right(e).wait_send()


def smooth_kernel(dims, starts, place, images, out, field, dist):
    shots, rows, layers, span, cells = dims
    for s in range(shots):
        window = images[s].reshape(rows * layers, span)
        if cells > span:
            window = jnp.concatenate([window, jnp.zeros((rows * layers, cells - span), F32)], axis=1)
        window = pltpu.roll(window, starts[s] * CX, 1)
        for c in range(cells // 128):
            piece = window[:, c * 128 : (c + 1) * 128]
            if s == 0:
                field[c] = piece
            else:
                field[c] += piece
    dist[...] = jnp.abs(
        lax.broadcasted_iota(jnp.int32, (cells, cells), 0) - lax.broadcasted_iota(jnp.int32, (cells, cells), 1)
    ).astype(F32)

    @pl.loop(0, layers)
    def _(z):
        depth_value = (place[0] * layers + z).astype(F32)
        length = CX * (1.5 + 4.5 * depth_value / (NZ - 1.0))
        rate = -1.0 / jnp.full((8, 128), length, F32)
        rate = rate[0:1, 0:1]
        weights = jnp.exp(dist[...] * rate)
        norm = jnp.sum(weights, axis=0, keepdims=True)
        w_hi, w_lo = split(weights)
        layer = jnp.concatenate(
            [field[c, pl.ds(z, rows, stride=layers), :] for c in range(cells // 128)], axis=1
        )
        f_hi, f_lo = split(layer)
        main = dot(jnp.concatenate([f_hi, f_lo], axis=0), w_hi)
        total = main[0:rows] + main[rows:] + dot(f_hi, w_lo)
        out[z] = total / norm


def on_device(
    velocity, log_density, fwd_prev, fwd_now, adj_now, adj_next,
    wavelet, source_pos, receiver_pos, observed, footprint, owner,
):
    shot = lax.axis_index("gx")
    column_index = lax.axis_index("gy")
    block_count = lax.axis_size("gx")
    block_cells, rows, depth = velocity.shape[1:]
    slots = footprint.shape[1]
    span = slots * block_cells
    half = span // 2
    speeds = lax.all_gather(velocity, "gx", axis=0, tiled=True)
    densities = lax.all_gather(log_density, "gx", axis=0, tiled=True)
    blocks = footprint[shot]
    holders = owner[jnp.maximum(blocks, 0)]
    speed = speeds[holders].reshape(span * rows, depth)
    dens = densities[holders].reshape(span * rows, depth)
    mask = jnp.broadcast_to(
        jnp.repeat((blocks >= 0).astype(F32), block_cells)[:, None], (span, depth)
    )
    spot = source_pos[0] - jnp.stack([jnp.int32(0), column_index * rows, jnp.int32(0)])
    scal = jnp.concatenate([spot.astype(F32), wavelet[0]])
    rec_y = receiver_pos[0, 1] - column_index * rows
    valid = (rec_y >= 0) & (rec_y < rows)
    code = jnp.where(valid, rec_y * half + receiver_pos[0, 0], -1)
    nrec = code.shape[0]
    first_x, second_x = band(span)
    first_z, second_z = band(depth)
    dx = jnp.asarray(np.concatenate([first_x, second_x], 0), BF)
    one = np.concatenate([first_z.T, second_z.T], 1)
    mz = jnp.asarray(np.concatenate([one, one], 0), BF)
    flat = lambda a: a.reshape(span * rows, depth)
    vm = pl.BlockSpec(memory_space=pltpu.VMEM)
    padded = pltpu.VMEM((rows + 2 * H, span, depth), F32)
    out = pl.pallas_call(
        functools.partial(wave_kernel, (rows, span, depth)),
        out_shape=jax.ShapeDtypeStruct((rows, depth, span), F32),
        in_specs=[pl.BlockSpec(memory_space=pltpu.SMEM)] + [vm] * 13,
        out_specs=vm,
        scratch_shapes=[
            padded, padded, padded, padded, padded, padded,
            pltpu.VMEM((NT, rows * span, depth), F32),
            pltpu.VMEM((rows, span, depth), F32),
            pltpu.VMEM((3, rows, span, depth), F32),
            pltpu.VMEM((rows + 2 * H, span, depth), BF),
            pltpu.VMEM((rows, nrec, half), BF),
            pltpu.VMEM((rows, half, nrec), BF),
            pltpu.VMEM((span, depth), F32),
            pltpu.VMEM((nrec, depth), F32),
            pltpu.VMEM((NT, nrec, 2 * depth), BF),
            pltpu.SemaphoreType.DMA((7, 2)),
            pltpu.SemaphoreType.DMA((7, 2)),
        ],
        compiler_params=pltpu.CompilerParams(
            collective_id=0, has_side_effects=True, vmem_limit_bytes=60 * 1024 * 1024
        ),
        name="wave",
    )(
        scal, flat(fwd_prev), flat(fwd_now), flat(adj_now), flat(adj_next), speed, dens, mask,
        code[:, None], code[None, :], receiver_pos[0, 2][:, None], observed[0][:, :, None], dx, mz,
    )
    layers = depth // block_count
    received = lax.all_to_all(out, "gx", split_axis=1, concat_axis=0, tiled=True)
    received = received.reshape(block_count, rows, layers, span)
    cells = block_count * block_cells
    shots = footprint.shape[0]
    sm = pl.BlockSpec(memory_space=pltpu.SMEM)
    return pl.pallas_call(
        functools.partial(smooth_kernel, (shots, rows, layers, span, cells)),
        out_shape=jax.ShapeDtypeStruct((layers, rows, cells), F32),
        in_specs=[sm, sm, vm],
        out_specs=vm,
        scratch_shapes=[
            pltpu.VMEM((cells // 128, rows * layers, 128), F32),
            pltpu.VMEM((cells, cells), F32),
        ],
        compiler_params=pltpu.CompilerParams(vmem_limit_bytes=56 * 1024 * 1024),
        name="smooth",
    )(footprint[:, 0], shot[None], received)


def solution(mesh):
    shared = P(("grp", "gx"), None, "gy", None)
    placed = (shared,) * 6 + (
        P(("grp", "gx"), None),
        P(("grp", "gx"), None),
        P(("grp", "gx"), None, None),
        P(("grp", "gx"), None, None),
        P("grp", None),
        P(),
    )
    return jax.shard_map(
        on_device,
        mesh=mesh,
        in_specs=placed,
        out_specs=P(("grp", "gx"), "gy", None),
        check_vma=False,
    )
```

time: 870 us -> 221 us (0.25); the launches traced: 858 us -> 221 us
  other arithmetic: 540 us -> 4.14 us
  Pallas kernels: 0 us -> 89.7 us
  loops' own time: 74.1 us -> 0 us
  local copies, waits for them, and re-layouts: 72.7 us -> 17.8 us
  starting transfers between devices: 43.3 us -> 3.78 us
  matrix products: 33.3 us -> 0 us
  waiting for transfers between devices: 80.4 us -> 91.8 us
    add x6 -> x0, other arithmetic: 376 us -> none  [the longest x3 191 us: on_device(): newer = 2.0 * current - older + apply(current) + wavelet[0, tick] * source]
    scatter-add x3 -> x0, other arithmetic: 101 us -> none  [on_device(): inject = jnp.zeros(extent, jnp.float32).at[rec_x, rec_y, rec_z].add(jnp.w...]
    pallas_call x0 -> x2, Pallas kernels: none -> 89.7 us  [the longest x1 80.2 us: on_device(): pl.pallas_call(functools.partial(wave_kernel, (rows, span, depth)), out_s...]
    another operation x1 -> x0, loops' own time: 74.1 us -> none  [on_device(): return lax.map(smooth_layer, jnp.arange(layers))]
    concatenate x7 -> x1, other arithmetic: 49.5 us -> 1.29 us  [on_device(): scal = jnp.concatenate([spot.astype(F32), wavelet[0]])]
    ppermute x14 -> x0, starting transfers between devices: 39.4 us -> none  [the longest x7 22.5 us: padded_2(): lax.ppermute(lax.slice_in_dim(block, block.shape[dim] - width, None, axis...]
    dot_general x33 -> x0, matrix products: 33.3 us -> none  [the longest x32 32.6 us: smooth_layer(): return jnp.dot(kernel, column, precision=lax.Precision.HIGHEST).T]
    all_gather x2, waiting for transfers between devices: 22.9 us -> 48.8 us  [the longest x1 26.1 us: on_device(): speeds = lax.all_gather(velocity, 'gx', axis=0, tiled=True)]
  transfers between devices with their start and end apart: 17 -> 3, of which waited for: 5 -> 3; matrix products, arithmetic and copies ran while one was open for 29% -> 5% of each run, Pallas kernels for 0% -> 0%
where the time goes in v1:
time: 221 us
  waiting for transfers between devices  91.8 us (42%)
  Pallas kernels  89.7 us (41%)
  local copies, waits for them, and re-layouts  17.8 us (8%)
  between operations  13.4 us (6%)
  other arithmetic  4.14 us (2%)
  starting transfers between devices  3.78 us (2%)
    pallas_call x1, Pallas kernels, on_device(): pl.pallas_call(functools.partial(wave_kernel, (rows, span, depth)), out_s...  80.2 us
    all_to_all x1, waiting for transfers between devices, on_device(): lax.all_to_all(out, 'gx', split_axis=1, concat_axis=0, tiled=True)  41.6 us
    all_gather x1, waiting for transfers between devices, on_device(): speeds = lax.all_gather(velocity, 'gx', axis=0, tiled=True)  26.1 us
    all_gather x1, waiting for transfers between devices, on_device(): densities = lax.all_gather(log_density, 'gx', axis=0, tiled=True)  22.7 us
    pallas_call x1, Pallas kernels, on_device(): pl.pallas_call(functools.partial(smooth_kernel, (shots, rows, layers, spa...  9.52 us
  transfers between devices with their start and end apart: 3, of which 3 were waited for; matrix products, arithmetic and copies ran while one was open for 5% of the time, Pallas kernels for 0%

profile of v1, /device:TPU:1, one launch (start us, length us, event | category | flops | bytes accessed | tf_op | source)
XLA Modules:
  0.0 220.8 jit_solution(10323415181375259979)
XLA Ops:
  6.5 0.0 copy-start
  6.5 0.0 all-gather.5.cloned.1.call-start
  6.5 0.7 all-gather.5.cloned.1.call-update
  7.3 0.0 all-gather.3.cloned.1.call-start
  7.3 0.7 all-gather.3.cloned.1.call-update
  8.0 0.7 fusion
  8.7 0.1 broadcast_in_dim.23
  8.8 0.1 broadcast_in_dim.24
  8.9 0.7 slice_bitcast_fusion
  9.6 0.0 copy-start.1
  9.6 0.8 copy.19.code_col
  10.4 0.8 copy.20.recz
  11.2 1.6 copy.21.obs
  12.8 0.7 maximum_bitcast_fusion
  13.5 0.0 copy-done
  13.5 0.6 gather_fusion
  14.1 0.7 fusion.2
  14.9 1.3 pad_maximum_fusion.scal
  16.2 22.7 %all-gather.5.cloned.1.call-done = bf16[4,64,16,128]{3,2,1,0:T(8,128)(2,1)} async-done(((bf16[1,64,16,128]{3,2,1,0:T(8,128)(2,1)}), bf16[4,64,16,128]{3,2,1,0:T(8,128)(2,1)}) %all-gather.5.cloned.1.call-update) | async-done | bytes 1048592 | tf_op jit(solution)/shard_map/all_gather | solution.py:329
  38.8 2.9 %gather_fusion.2 = bf16[4,64,16,128]{3,2,1,0:T(8,128)(2,1)} fusion(bf16[4,64,16,128]{3,2,1,0:T(8,128)(2,1)} %all-gather.5.cloned.1.call-done, s32[1024]{0:T(1024)S(1)} %pad_clamp_fusion), kind=kCustom, calls=%fused_computation.2 | custom fusion | bytes 2097168 | tf_op jit(solution)/shard_map/gather | solution.py:333
  41.7 26.1 %all-gather.3.cloned.1.call-done = bf16[4,64,16,128]{3,2,1,0:T(8,128)(2,1)} async-done(((bf16[1,64,16,128]{3,2,1,0:T(8,128)(2,1)}), bf16[4,64,16,128]{3,2,1,0:T(8,128)(2,1)}) %all-gather.3.cloned.1.call-update) | async-done | bytes 1048592 | tf_op jit(solution)/shard_map/all_gather | solution.py:328
  67.9 2.9 %gather_fusion.1 = bf16[4,64,16,128]{3,2,1,0:T(8,128)(2,1)} fusion(bf16[4,64,16,128]{3,2,1,0:T(8,128)(2,1)} %all-gather.3.cloned.1.call-done, s32[1024]{0:T(1024)S(1)} %pad_clamp_fusion), kind=kCustom, calls=%fused_computation.1 | custom fusion | bytes 2097168 | tf_op jit(solution)/shard_map/gather | solution.py:332
  70.8 0.0 copy-done.1
  70.8 0.8 broadcast_in_dim.25.maskp
  71.5 80.2 %wave.1 = f32[16,128,256]{2,1,0:T(8,128)} custom-call(f32[6]{0:T(128)} %pad_maximum_fusion.scal, bf16[4096,128]{1,0:T(8,128)(2,1)} %bitcast.32, bf16[4096,128]{1,0:T(8,128)(2,1)} %bitcast.33, bf16[4096,128]{1,0:T(8,128)(2,1)} %bitcast.34, bf16[4096,128]{1,0:T(8,128)(2,1)} %bitcast.35, bf16[4096,128]{1,0:T(8,128)(2,1)} %bitcast.31, ...), custom_call_target="tpu_custom_call" | custom-call | tf_op jit(solution)/shard_map/wave/pallas_call | solution.py:351
  151.7 4.1 %copy.22 = f32[16,128,256]{2,0,1:T(8,128)} copy(f32[16,128,256]{2,1,0:T(8,128)} %wave.1) | data formatting | bytes 4194304 | tf_op jit(solution)/shard_map/wave/pallas_call | solution.py:351
  155.9 0.0 copy-start.2
  155.9 3.7 %all-to-all-start = ((f32[16,128,256]{2,0,1:T(8,128)}), f32[16,128,256]{2,0,1:T(8,128)S(1)}, u32[]{:S(2)}, u32[]{:S(2)}) async-start(f32[16,128,256]{2,0,1:T(8,128)} %copy.22), calls=%async_computation | async-start | bytes 4194304 | tf_op jit(solution)/shard_map/all_to_all | solution.py:379
  159.6 0.0 copy-done.2
  159.6 0.6 slice_reduce_fusion.starts
  160.2 41.6 %all-to-all-done = f32[16,128,256]{2,0,1:T(8,128)S(1)} async-done(((f32[16,128,256]{2,0,1:T(8,128)}), f32[16,128,256]{2,0,1:T(8,128)S(1)}, u32[]{:S(2)}, u32[]{:S(2)}) %all-to-all-start) | async-done | bytes 2097184 | tf_op jit(solution)/shard_map/all_to_all | solution.py:379
  201.8 2.6 %copy.28 = f32[16,4,32,256]{3,2,0,1:T(8,128)} copy(f32[16,4,32,256]{3,0,2,1:T(8,128)S(1)} %bitcast.28) | data formatting | bytes 4194304 | tf_op jit(solution)/shard_map/all_to_all | solution.py:379
  204.4 9.5 %smooth.1 = f32[32,16,256]{2,1,0:T(8,128)} custom-call(s32[4]{0:T(128)} %slice_reduce_fusion.starts, s32[1]{0:T(128)} %bitcast.place, f32[4,16,32,256]{3,2,1,0:T(8,128)} %bitcast.29), custom_call_target="tpu_custom_call" | custom-call | tf_op jit(solution)/shard_map/smooth/pallas_call | solution.py:384
  (3 shorter events, 0.0 us)
Async XLA Ops:
  6.5 6.9 %copy-start = (s32[4]{0:T(128)S(1)}, s32[4]{0:T(128)}, u32[]{:S(2)}) copy-start(s32[4]{0:T(128)} %param.25) | copy-start | bytes 52
  6.5 32.3 %all-gather.5.cloned.1.call-start = ((), (), s32[]{:S(2)}) async-start(), calls=%async_computation.2 | async-start | bytes 1310720 | tf_op jit(solution)/shard_map/all_gather | solution.py:329
  7.3 60.6 %all-gather.3.cloned.1.call-start = ((), (), s32[]{:S(2)}) async-start(), calls=%async_computation.1 | async-start | bytes 1310720 | tf_op jit(solution)/shard_map/all_gather | solution.py:328
  9.6 61.2 %copy-start.1 = (s32[1,1,256]{2,0,1:T(1,128)}, s32[1,1,256]{2,0,1:T(1,128)S(1)}, u32[]{:S(2)}) copy-start(s32[1,1,256]{2,0,1:T(1,128)S(1)} %get-tuple-element.6) | copy-start | bytes 3076
  155.9 3.8 %copy-start.2 = (s32[4,4]{1,0:T(4,128)S(1)}, s32[4,4]{1,0:T(4,128)}, u32[]{:S(2)}) copy-start(s32[4,4]{1,0:T(4,128)} %param.24) | copy-start | bytes 196
  155.9 46.0 %all-to-all-start = ((f32[16,128,256]{2,0,1:T(8,128)}), f32[16,128,256]{2,0,1:T(8,128)S(1)}, u32[]{:S(2)}, u32[]{:S(2)}) async-start(f32[16,128,256]{2,0,1:T(8,128)} %copy.22), calls=%async_computation | async-start | bytes 4194304 | tf_op jit(solution)/shard_map/all_to_all | solution.py:379
Sparse Core Ops, SparseCore 0:
  8.9 29.8 all-gather.4
  40.4 27.4 all-gather.2

commit v2 on v1

--- a/solution.py
+++ b/solution.py
@@ -40,20 +40,30 @@
 
 def wave_kernel(
     dims,
-    scal, fprev, fnow, anow, anext, speed, dens, maskp, code_col, code_row, recz, obs, dx, mz,
+    source_pos, wavelet, footprint, owner,
+    fprev, fnow, anow, anext, speed, dens, receivers, observed, dx, mz,
     out,
     p0, p1, p2, q3, q2, q1, acc, sq, grad, den, xt, xo, hot, vsum, inj,
-    send_sem, recv_sem,
+    model_d, model_s, maskp, obs, recz, outb,
+    send_sem, recv_sem, model_send, model_recv, image_send, image_recv, own_sem,
 ):
-    rows, span, depth = dims
+    rows, span, depth, cells = dims
     half = span // 2
+    gx = lax.axis_index("gx")
+    lanes_gx = lax.axis_size("gx")
     gy = lax.axis_index("gy")
     count = lax.axis_size("gy")
+    layers = depth // lanes_gx
     has_left = gy > 0
     has_right = gy < count - 1
     barrier = pltpu.get_barrier_semaphore()
     steps = (den, p0, q3, p1, p2, q2, q1)
 
+    for d in range(1, lanes_gx):
+        pl.semaphore_signal(
+            barrier, inc=1, device_id={"gx": lax.rem(gx + d, lanes_gx)}, device_id_type=pl.DeviceIdType.MESH
+        )
+
     @pl.when(has_left)
     def _():
         pl.semaphore_signal(barrier, inc=1, device_id={"gy": gy - 1}, device_id_type=pl.DeviceIdType.MESH)
@@ -61,6 +71,10 @@
     @pl.when(has_right)
     def _():
         pl.semaphore_signal(barrier, inc=1, device_id={"gy": gy + 1}, device_id_type=pl.DeviceIdType.MESH)
+
+    model = (model_d, model_s)
+    model_d[gx] = dens[...]
+    model_s[gx] = speed[...]
 
     @pl.when(jnp.logical_not(has_left))
     def _():
@@ -72,7 +86,51 @@
         for buf in steps:
             buf[rows + H : rows + 2 * H] = jnp.zeros((H, span, depth), buf.dtype)
 
-    pl.semaphore_wait(barrier, has_left.astype(jnp.int32) + has_right.astype(jnp.int32))
+    pl.semaphore_wait(
+        barrier, lanes_gx - 1 + has_left.astype(jnp.int32) + has_right.astype(jnp.int32)
+    )
+
+    def up_copy(a, r, block):
+        return pltpu.make_async_remote_copy(
+            src_ref=model[a].at[block], dst_ref=model[a].at[block],
+            send_sem=model_send.at[a, 0, r], recv_sem=model_recv.at[a, 0, r],
+            device_id={"gx": gx + 1}, device_id_type=pl.DeviceIdType.MESH)
+
+    def down_copy(a, r, block):
+        return pltpu.make_async_remote_copy(
+            src_ref=model[a].at[block], dst_ref=model[a].at[block],
+            send_sem=model_send.at[a, 1, r], recv_sem=model_recv.at[a, 1, r],
+            device_id={"gx": gx - 1}, device_id_type=pl.DeviceIdType.MESH)
+
+    def pass_on(a, r):
+        @pl.when((gx - r >= 0) & (gx + 1 < lanes_gx))
+        def _():
+            up_copy(a, r, gx - r).start()
+
+        @pl.when((gx + r < lanes_gx) & (gx >= 1))
+        def _():
+            down_copy(a, r, gx + r).start()
+
+    def passed(a, r):
+        @pl.when((gx - r >= 0) & (gx + 1 < lanes_gx))
+        def _():
+            up_copy(a, r, gx - r).wait_send()
+
+        @pl.when((gx + r < lanes_gx) & (gx >= 1))
+        def _():
+            down_copy(a, r, gx + r).wait_send()
+
+    def arrive(a, r):
+        @pl.when(gx - 1 - r >= 0)
+        def _():
+            up_copy(a, r, gx - 1 - r).wait_recv()
+
+        @pl.when(gx + 1 + r < lanes_gx)
+        def _():
+            down_copy(a, r, gx + 1 + r).wait_recv()
+
+    pass_on(0, 0)
+    pass_on(1, 0)
 
     def to_left(e):
         buf = steps[e]
@@ -113,6 +171,12 @@
         def _(y):
             put(y, acc[0, pl.ds(y, span, stride=rows), :])
 
+    slots = footprint.shape[1]
+    block_rows = dens.shape[0]
+    lives = [footprint[gx, j] for j in range(slots)]
+    for j in range(slots):
+        live = jnp.where(lives[j] >= 0, 1.0, 0.0)
+        maskp[j * cells : (j + 1) * cells] = jnp.full((cells, depth), live, F32)
     mask = maskp[...]
 
     def into(buf):
@@ -123,35 +187,69 @@
     def put_speed(y, u):
         sq[y] = u * u * mask * (1.0 / 5040.0)
 
-    turn(dens, into(den))
-    send(0)
+    def gather(a, put):
+        for j in range(slots):
+            holder = owner[jnp.maximum(lives[j], 0)]
+            acc[0, j * block_rows : (j + 1) * block_rows] = model[a][holder].astype(F32)
+
+        @pl.loop(0, rows)
+        def _(y):
+            put(y, acc[0, pl.ds(y, span, stride=rows), :])
+
     turn(fnow, into(p0))
     send(1)
     turn(anow, into(q3))
     send(2)
-    turn(fprev, into(p1))
-    turn(anext, into(q2))
-    turn(speed, put_speed)
-
-    source_x, source_y, source_z = scal[0], scal[1], scal[2]
+
+    def onward(r):
+        for a in range(2):
+            arrive(a, r - 1)
+            pass_on(a, r)
+
+    nrec = receivers.shape[1]
+
+    def column(row):
+        return jnp.broadcast_to(row.astype(F32), (depth, nrec)).T
+
+    for t in range(NT):
+        obs[t] = column(observed[t : t + 1, :])
+    recz[...] = column(receivers[2:3, :])
+    rec_y = receivers[1:2, :] - gy * rows
+    valid = (rec_y >= 0) & (rec_y < rows)
+    code_row = jnp.where(valid, rec_y * half + receivers[0:1, :], -1)
+    code_col = column(code_row)
+    source_x = source_pos[0, 0].astype(F32)
+    source_y = (source_pos[0, 1] - gy * rows).astype(F32)
+    source_z = source_pos[0, 2].astype(F32)
     at_x = lax.broadcasted_iota(jnp.int32, (span, depth), 0).astype(F32) == source_x
     at_z = lax.broadcasted_iota(jnp.int32, (span, depth), 1).astype(F32) == source_z
     hot[...] = jnp.where(at_x & at_z, mask, 0.0)
-    nrec = recz.shape[0]
     mask2 = jnp.concatenate([mask[:half]] * (nrec // depth), axis=1)
+    code_lanes = jnp.concatenate([code_col] * (half // depth), axis=1)
 
     @pl.loop(0, rows)
     def _(y):
-        lanes = lax.broadcasted_iota(jnp.int32, (nrec, half), 1) + y * half
-        xt[y] = jnp.where(lanes == code_col[...], 1.0, 0.0).astype(BF)
+        lanes = (lax.broadcasted_iota(jnp.int32, (nrec, half), 1) + y * half).astype(F32)
+        xt[y] = jnp.where(lanes == code_lanes, 1.0, 0.0).astype(BF)
         subs = lax.broadcasted_iota(jnp.int32, (half, nrec), 0) + y * half
-        xo[y] = jnp.where(subs == code_row[...], mask2, 0.0).astype(BF)
-
-    def planes(first, receive_from, body):
+        xo[y] = jnp.where(subs == code_row, mask2, 0.0).astype(BF)
+
+    onward(1)
+    turn(fprev, into(p1))
+    turn(anext, into(q2))
+    for r in range(2, lanes_gx - 1):
+        onward(r)
+    arrive(0, lanes_gx - 2)
+    gather(0, into(den))
+    send(0)
+
+    def planes(first, receive_from, body, after=None):
         @pl.loop(H, rows - H)
         def _(y):
             body(y)
 
+        if after is not None:
+            after()
         receive(receive_from)
 
         @pl.loop(0, 2 * H)
@@ -168,6 +266,8 @@
         grad[1, y] = total * (6.0 / 840.0)
 
     planes(0, 0, slope)
+    arrive(1, lanes_gx - 2)
+    gather(1, put_speed)
 
     def spatial(buf, y, exact, finish):
         u = buf[y + H]
@@ -211,7 +311,7 @@
         vsum[...] = jnp.zeros_like(vsum)
 
         def forward(y, t=t, cur=cur):
-            amount = jnp.where(y.astype(F32) == source_y, scal[3 + t], 0.0)
+            amount = jnp.where(y.astype(F32) == source_y, wavelet[0, t], 0.0)
             pieces = []
 
             def finish(r, rs, center, lu):
@@ -231,11 +331,37 @@
         planes(0, (1, 3, 4)[t], forward)
         if t < NT - 1:
             send(3 + t)
-        here = lax.broadcasted_iota(jnp.int32, (nrec, depth), 1) == recz[...]
+        here = lax.broadcasted_iota(jnp.int32, (nrec, depth), 1).astype(F32) == recz[...]
         residual = jnp.where(here, vsum[...] - obs[t], 0.0)
         hi, lo = split(residual)
         inj[t, :, 0:depth] = hi
         inj[t, :, depth:] = lo
+
+    parts = ((H, rows - 2 * H), (0, H), (rows - H, H))
+
+    def image_copy(d, part, target):
+        start, size = parts[part]
+        return pltpu.make_async_remote_copy(
+            src_ref=outb.at[pl.ds(start, size), pl.ds(pl.multiple_of(target * layers, layers), layers), :],
+            dst_ref=out.at[gx, pl.ds(start, size)],
+            send_sem=image_send.at[d, part], recv_sem=image_recv.at[d, part],
+            device_id={"gx": target}, device_id_type=pl.DeviceIdType.MESH)
+
+    def deliver(part):
+        for d in range(1, lanes_gx):
+            image_copy(d, part, lax.rem(gx + d, lanes_gx)).start()
+
+    def delivered(part):
+        for d in range(1, lanes_gx):
+            copy = image_copy(d, part, lax.rem(gx + d, lanes_gx))
+            copy.wait_send()
+            start, size = parts[part]
+            came = lax.rem(gx + lanes_gx - d, lanes_gx)
+            pltpu.make_async_remote_copy(
+                src_ref=outb.at[pl.ds(start, size), pl.ds(pl.multiple_of(gx * layers, layers), layers), :],
+                dst_ref=out.at[came, pl.ds(start, size)],
+                send_sem=image_send.at[d, part], recv_sem=image_recv.at[d, part],
+                device_id={"gx": came}, device_id_type=pl.DeviceIdType.MESH).wait_recv()
 
     adjoint = {3: q3, 2: q2, 1: q1}
     for t in reversed(range(NT)):
@@ -263,12 +389,21 @@
 
             spatial(cur, y, t == NT - 1, finish)
             if t == 0:
-                out[y] = jnp.concatenate(images, axis=0).T
-
-        planes(0, (6, 5, 2)[t], backward)
+                outb[y] = jnp.concatenate(images, axis=0).T
+
+        planes(0, (6, 5, 2)[t], backward, None if t > 0 else functools.partial(deliver, 0))
         if t > 0:
             send(5 + NT - 1 - t)
 
+    deliver(1)
+    deliver(2)
+    own = pltpu.make_async_copy(
+        outb.at[:, pl.ds(pl.multiple_of(gx * layers, layers), layers), :], out.at[gx], own_sem
+    )
+    own.start()
+    for r in range(lanes_gx - 1):
+        passed(0, r)
+        passed(1, r)
     for e in range(7):
         @pl.when(has_left)
         def _():
@@ -278,14 +413,19 @@
         def _():
             to_right(e).wait_send()
 
-
-def smooth_kernel(dims, starts, place, images, out, field, dist):
+    own.wait()
+    for part in range(len(parts)):
+        delivered(part)
+
+
+def smooth_kernel(dims, footprint, images, out, field, dist):
     shots, rows, layers, span, cells = dims
+    place = lax.axis_index("gx")
     for s in range(shots):
         window = images[s].reshape(rows * layers, span)
         if cells > span:
             window = jnp.concatenate([window, jnp.zeros((rows * layers, cells - span), F32)], axis=1)
-        window = pltpu.roll(window, starts[s] * CX, 1)
+        window = pltpu.roll(window, footprint[s, 0] * CX, 1)
         for c in range(cells // 128):
             piece = window[:, c * 128 : (c + 1) * 128]
             if s == 0:
@@ -298,7 +438,7 @@
 
     @pl.loop(0, layers)
     def _(z):
-        depth_value = (place[0] * layers + z).astype(F32)
+        depth_value = (place * layers + z).astype(F32)
         length = CX * (1.5 + 4.5 * depth_value / (NZ - 1.0))
         rate = -1.0 / jnp.full((8, 128), length, F32)
         rate = rate[0:1, 0:1]
@@ -318,41 +458,27 @@
     velocity, log_density, fwd_prev, fwd_now, adj_now, adj_next,
     wavelet, source_pos, receiver_pos, observed, footprint, owner,
 ):
-    shot = lax.axis_index("gx")
-    column_index = lax.axis_index("gy")
     block_count = lax.axis_size("gx")
     block_cells, rows, depth = velocity.shape[1:]
-    slots = footprint.shape[1]
+    shots, slots = footprint.shape
     span = slots * block_cells
     half = span // 2
-    speeds = lax.all_gather(velocity, "gx", axis=0, tiled=True)
-    densities = lax.all_gather(log_density, "gx", axis=0, tiled=True)
-    blocks = footprint[shot]
-    holders = owner[jnp.maximum(blocks, 0)]
-    speed = speeds[holders].reshape(span * rows, depth)
-    dens = densities[holders].reshape(span * rows, depth)
-    mask = jnp.broadcast_to(
-        jnp.repeat((blocks >= 0).astype(F32), block_cells)[:, None], (span, depth)
-    )
-    spot = source_pos[0] - jnp.stack([jnp.int32(0), column_index * rows, jnp.int32(0)])
-    scal = jnp.concatenate([spot.astype(F32), wavelet[0]])
-    rec_y = receiver_pos[0, 1] - column_index * rows
-    valid = (rec_y >= 0) & (rec_y < rows)
-    code = jnp.where(valid, rec_y * half + receiver_pos[0, 0], -1)
-    nrec = code.shape[0]
+    layers = depth // block_count
+    nrec = receiver_pos.shape[2]
     first_x, second_x = band(span)
     first_z, second_z = band(depth)
     dx = jnp.asarray(np.concatenate([first_x, second_x], 0), BF)
     one = np.concatenate([first_z.T, second_z.T], 1)
     mz = jnp.asarray(np.concatenate([one, one], 0), BF)
-    flat = lambda a: a.reshape(span * rows, depth)
+    flat = lambda a: a.reshape(a.shape[1] * rows, depth)
     vm = pl.BlockSpec(memory_space=pltpu.VMEM)
+    sm = pl.BlockSpec(memory_space=pltpu.SMEM)
     padded = pltpu.VMEM((rows + 2 * H, span, depth), F32)
-    out = pl.pallas_call(
-        functools.partial(wave_kernel, (rows, span, depth)),
-        out_shape=jax.ShapeDtypeStruct((rows, depth, span), F32),
-        in_specs=[pl.BlockSpec(memory_space=pltpu.SMEM)] + [vm] * 13,
-        out_specs=vm,
+    received = pl.pallas_call(
+        functools.partial(wave_kernel, (rows, span, depth, block_cells)),
+        out_shape=jax.ShapeDtypeStruct((block_count, rows, layers, span), F32),
+        in_specs=[sm] * 4 + [vm] * 10,
+        out_specs=pl.BlockSpec(memory_space=pl.ANY),
         scratch_shapes=[
             padded, padded, padded, padded, padded, padded,
             pltpu.VMEM((NT, rows * span, depth), F32),
@@ -364,27 +490,34 @@
             pltpu.VMEM((span, depth), F32),
             pltpu.VMEM((nrec, depth), F32),
             pltpu.VMEM((NT, nrec, 2 * depth), BF),
+            pltpu.VMEM((block_count, block_cells * rows, depth), BF),
+            pltpu.VMEM((block_count, block_cells * rows, depth), BF),
+            pltpu.VMEM((span, depth), F32),
+            pltpu.VMEM((NT, nrec, depth), F32),
+            pltpu.VMEM((nrec, depth), F32),
+            pltpu.VMEM((rows, depth, span), F32),
             pltpu.SemaphoreType.DMA((7, 2)),
             pltpu.SemaphoreType.DMA((7, 2)),
+            pltpu.SemaphoreType.DMA((2, 2, block_count)),
+            pltpu.SemaphoreType.DMA((2, 2, block_count)),
+            pltpu.SemaphoreType.DMA((block_count, 3)),
+            pltpu.SemaphoreType.DMA((block_count, 3)),
+            pltpu.SemaphoreType.DMA,
         ],
         compiler_params=pltpu.CompilerParams(
             collective_id=0, has_side_effects=True, vmem_limit_bytes=60 * 1024 * 1024
         ),
         name="wave",
     )(
-        scal, flat(fwd_prev), flat(fwd_now), flat(adj_now), flat(adj_next), speed, dens, mask,
-        code[:, None], code[None, :], receiver_pos[0, 2][:, None], observed[0][:, :, None], dx, mz,
+        source_pos, wavelet, footprint, owner,
+        flat(fwd_prev), flat(fwd_now), flat(adj_now), flat(adj_next), flat(velocity), flat(log_density),
+        receiver_pos[0], observed[0], dx, mz,
     )
-    layers = depth // block_count
-    received = lax.all_to_all(out, "gx", split_axis=1, concat_axis=0, tiled=True)
-    received = received.reshape(block_count, rows, layers, span)
     cells = block_count * block_cells
-    shots = footprint.shape[0]
-    sm = pl.BlockSpec(memory_space=pltpu.SMEM)
     return pl.pallas_call(
         functools.partial(smooth_kernel, (shots, rows, layers, span, cells)),
         out_shape=jax.ShapeDtypeStruct((layers, rows, cells), F32),
-        in_specs=[sm, sm, vm],
+        in_specs=[sm, vm],
         out_specs=vm,
         scratch_shapes=[
             pltpu.VMEM((cells // 128, rows * layers, 128), F32),
@@ -392,7 +525,7 @@
         ],
         compiler_params=pltpu.CompilerParams(vmem_limit_bytes=56 * 1024 * 1024),
         name="smooth",
-    )(footprint[:, 0], shot[None], received)
+    )(footprint, received)
 
 
 def solution(mesh):

time: 221 us -> 144 us (0.65)
  waiting for transfers between devices: 91.8 us -> 0 us
  Pallas kernels: 89.7 us -> 141 us
  local copies, waits for them, and re-layouts: 17.8 us -> 2.56 us
  between operations: 13.4 us -> 0.01 us
  other arithmetic: 4.14 us -> 0 us
  starting transfers between devices: 3.78 us -> 0 us
    pallas_call x1, Pallas kernels: 80.2 us -> 132 us  [on_device(): pl.pallas_call(functools.partial(wave_kernel, (rows, span, depth, block_c...]
    all_gather x2 -> x0, waiting for transfers between devices: 48.8 us -> none  [the longest x1 26.1 us: on_device(): speeds = lax.all_gather(velocity, 'gx', axis=0, tiled=True)]
    all_to_all x1 -> x0, waiting for transfers between devices: 41.6 us -> none  [on_device(): lax.all_to_all(out, 'gx', split_axis=1, concat_axis=0, tiled=True)]
    gather x3 -> x0, local copies, waits for them, and re-layouts: 6.42 us -> none  [the longest x1 2.9 us: on_device(): speed = speeds[holders].reshape(span * rows, depth)]
    pallas_call x1 -> x0, local copies, waits for them, and re-layouts: 4.13 us -> none  [on_device(): pl.pallas_call(functools.partial(wave_kernel, (rows, span, depth)), out_s...]
    all_to_all x1 -> x0, starting transfers between devices: 3.74 us -> none  [on_device(): lax.all_to_all(out, 'gx', split_axis=1, concat_axis=0, tiled=True)]
    all_to_all x1 -> x0, local copies, waits for them, and re-layouts: 2.56 us -> none  [on_device(): lax.all_to_all(out, 'gx', split_axis=1, concat_axis=0, tiled=True)]
    unnamed x6 -> x2, local copies, waits for them, and re-layouts: 0.01 us -> 2.56 us
  transfers between devices with their start and end apart: 3 -> 0, of which waited for: 3 -> 0; matrix products, arithmetic and copies ran while one was open for 5% -> 0% of each run, Pallas kernels for 0% -> 0%
where the time goes in v2:
time: 144 us
  Pallas kernels  141 us (98%)
  local copies, waits for them, and re-layouts  2.56 us (2%)
    pallas_call x1, Pallas kernels, on_device(): pl.pallas_call(functools.partial(wave_kernel, (rows, span, depth, block_c...  132 us
    pallas_call x1, Pallas kernels, on_device(): pl.pallas_call(functools.partial(smooth_kernel, (shots, rows, layers, spa...  9.42 us

profile of v2, /device:TPU:1, one launch (start us, length us, event | category | flops | bytes accessed | tf_op | source)
XLA Modules:
  0.0 144.0 jit_solution(297206565482214099)
XLA Ops:
  0.0 1.3 copy.20
  1.3 1.3 copy.19
  2.6 132.0 %wave.1.images = f32[4,16,32,256]{3,2,1,0:T(8,128)} custom-call(s32[1,3]{1,0:T(1,128)} %source_pos.1, f32[1,3]{1,0:T(1,128)} %wavelet.1, s32[4,4]{1,0:T(4,128)} %footprint.3, s32[4]{0:T(128)} %owner.1, bf16[4096,128]{1,0:T(8,128)(2,1)} %bitcast.12, bf16[4096,128]{1,0:T(8,128)(2,1)} %bitcast.13, bf16[4096,128]{1,0:T(8,128)(2,1)} %bitcast.14, ...), custom_call_target="tpu_custom_call" | custom-call | tf_op jit(solution)/shard_map/wave/pallas_call | solution.py:477
  134.6 9.4 %smooth.1 = f32[32,16,256]{2,1,0:T(8,128)} custom-call(s32[4,4]{1,0:T(4,128)} %footprint.3, f32[4,16,32,256]{3,2,1,0:T(8,128)} %wave.1.images), custom_call_target="tpu_custom_call" | custom-call | tf_op jit(solution)/shard_map/smooth/pallas_call | solution.py:517

commit v3 on v2

--- a/solution.py
+++ b/solution.py
@@ -42,10 +42,10 @@
     dims,
     source_pos, wavelet, footprint, owner,
     fprev, fnow, anow, anext, speed, dens, receivers, observed, dx, mz,
-    out,
+    out, tails,
     p0, p1, p2, q3, q2, q1, acc, sq, grad, den, xt, xo, hot, vsum, inj,
-    model_d, model_s, maskp, obs, recz, outb,
-    send_sem, recv_sem, model_send, model_recv, image_send, image_recv, own_sem,
+    model_d, model_s, maskp, obs, recz, outb, carry, tailb,
+    send_sem, recv_sem, model_send, model_recv, image_send, image_recv, own_sem, own_tail,
 ):
     rows, span, depth, cells = dims
     half = span // 2
@@ -339,29 +339,27 @@
 
     parts = ((H, rows - 2 * H), (0, H), (rows - H, H))
 
-    def image_copy(d, part, target):
-        start, size = parts[part]
+    def image_copy(d, part, target, source):
+        if part < len(parts):
+            start, size = parts[part]
+            src = outb.at[pl.ds(start, size), target]
+            dst = out.at[source, pl.ds(start, size)]
+        else:
+            src, dst = tailb.at[target], tails.at[source]
         return pltpu.make_async_remote_copy(
-            src_ref=outb.at[pl.ds(start, size), pl.ds(pl.multiple_of(target * layers, layers), layers), :],
-            dst_ref=out.at[gx, pl.ds(start, size)],
+            src_ref=src, dst_ref=dst,
             send_sem=image_send.at[d, part], recv_sem=image_recv.at[d, part],
             device_id={"gx": target}, device_id_type=pl.DeviceIdType.MESH)
 
     def deliver(part):
         for d in range(1, lanes_gx):
-            image_copy(d, part, lax.rem(gx + d, lanes_gx)).start()
+            image_copy(d, part, lax.rem(gx + d, lanes_gx), gx).start()
 
     def delivered(part):
         for d in range(1, lanes_gx):
-            copy = image_copy(d, part, lax.rem(gx + d, lanes_gx))
-            copy.wait_send()
-            start, size = parts[part]
+            image_copy(d, part, lax.rem(gx + d, lanes_gx), gx).wait_send()
             came = lax.rem(gx + lanes_gx - d, lanes_gx)
-            pltpu.make_async_remote_copy(
-                src_ref=outb.at[pl.ds(start, size), pl.ds(pl.multiple_of(gx * layers, layers), layers), :],
-                dst_ref=out.at[came, pl.ds(start, size)],
-                send_sem=image_send.at[d, part], recv_sem=image_recv.at[d, part],
-                device_id={"gx": came}, device_id_type=pl.DeviceIdType.MESH).wait_recv()
+            image_copy(d, part, came, came).wait_recv()
 
     adjoint = {3: q3, 2: q2, 1: q1}
     for t in reversed(range(NT)):
@@ -371,6 +369,7 @@
             added = dot(xo[y], inj[t])
             added = added[:, 0:depth] + added[:, depth:]
             images = []
+            left = []
 
             def finish(r, rs, center, lu):
                 old = q2[y + H, rs, :] if t == NT - 1 else adjoint[t + 2][y + H, rs, :]
@@ -385,11 +384,20 @@
                 if t > 0:
                     acc_rows(t, y, r)[...] = term
                 else:
-                    images.append(term)
+                    for k in range(0, CHUNK, 8):
+                        value = term[k : k + 8]
+                        if left:
+                            value = value + left.pop()
+                        kept = value.astype(BF).astype(F32)
+                        left.append(value - kept)
+                        images.append(kept)
 
             spatial(cur, y, t == NT - 1, finish)
             if t == 0:
-                outb[y] = jnp.concatenate(images, axis=0).T
+                turned = jnp.concatenate(images, axis=0).T
+                for g in range(lanes_gx):
+                    outb[y, g] = turned[g * layers : (g + 1) * layers].astype(BF)
+                carry[y] = left[0]
 
         planes(0, (6, 5, 2)[t], backward, None if t > 0 else functools.partial(deliver, 0))
         if t > 0:
@@ -397,10 +405,14 @@
 
     deliver(1)
     deliver(2)
-    own = pltpu.make_async_copy(
-        outb.at[:, pl.ds(pl.multiple_of(gx * layers, layers), layers), :], out.at[gx], own_sem
-    )
+    turned = carry[...].reshape(rows * 8, depth).T
+    for g in range(lanes_gx):
+        tailb[g] = turned[g * layers : (g + 1) * layers].astype(BF)
+    deliver(3)
+    own = pltpu.make_async_copy(outb.at[:, gx], out.at[gx], own_sem)
+    own_end = pltpu.make_async_copy(tailb.at[gx], tails.at[gx], own_tail)
     own.start()
+    own_end.start()
     for r in range(lanes_gx - 1):
         passed(0, r)
         passed(1, r)
@@ -414,15 +426,26 @@
             to_right(e).wait_send()
 
     own.wait()
-    for part in range(len(parts)):
+    own_end.wait()
+    for part in range(len(parts) + 1):
         delivered(part)
 
 
-def smooth_kernel(dims, footprint, images, out, field, dist):
+def smooth_kernel(dims, footprint, images, tails, out, field, dist):
     shots, rows, layers, span, cells = dims
     place = lax.axis_index("gx")
     for s in range(shots):
-        window = images[s].reshape(rows * layers, span)
+        window = images[s].astype(F32).reshape(rows * layers, span)
+        tail = tails[s].astype(F32)
+        width = tail.shape[1]
+        at_end = lax.broadcasted_iota(jnp.int32, tail.shape, 1) >= width - 8
+        ends = [
+            jnp.where(at_end, pltpu.roll(tail, width - 8 - 8 * y, 1) if y < rows - 1 else tail, 0.0)
+            for y in range(rows)
+        ]
+        window = jnp.concatenate(
+            [window[:, : span - width], window[:, span - width :] + jnp.concatenate(ends, axis=0)], axis=1
+        )
         if cells > span:
             window = jnp.concatenate([window, jnp.zeros((rows * layers, cells - span), F32)], axis=1)
         window = pltpu.roll(window, footprint[s, 0] * CX, 1)
@@ -474,11 +497,14 @@
     vm = pl.BlockSpec(memory_space=pltpu.VMEM)
     sm = pl.BlockSpec(memory_space=pltpu.SMEM)
     padded = pltpu.VMEM((rows + 2 * H, span, depth), F32)
-    received = pl.pallas_call(
+    received, tails = pl.pallas_call(
         functools.partial(wave_kernel, (rows, span, depth, block_cells)),
-        out_shape=jax.ShapeDtypeStruct((block_count, rows, layers, span), F32),
+        out_shape=(
+            jax.ShapeDtypeStruct((block_count, rows, layers, span), BF),
+            jax.ShapeDtypeStruct((block_count, layers, rows * 8), BF),
+        ),
         in_specs=[sm] * 4 + [vm] * 10,
-        out_specs=pl.BlockSpec(memory_space=pl.ANY),
+        out_specs=(pl.BlockSpec(memory_space=pl.ANY),) * 2,
         scratch_shapes=[
             padded, padded, padded, padded, padded, padded,
             pltpu.VMEM((NT, rows * span, depth), F32),
@@ -495,13 +521,16 @@
             pltpu.VMEM((span, depth), F32),
             pltpu.VMEM((NT, nrec, depth), F32),
             pltpu.VMEM((nrec, depth), F32),
-            pltpu.VMEM((rows, depth, span), F32),
+            pltpu.VMEM((rows, block_count, layers, span), BF),
+            pltpu.VMEM((rows, 8, depth), F32),
+            pltpu.VMEM((block_count, layers, rows * 8), BF),
             pltpu.SemaphoreType.DMA((7, 2)),
             pltpu.SemaphoreType.DMA((7, 2)),
             pltpu.SemaphoreType.DMA((2, 2, block_count)),
             pltpu.SemaphoreType.DMA((2, 2, block_count)),
-            pltpu.SemaphoreType.DMA((block_count, 3)),
-            pltpu.SemaphoreType.DMA((block_count, 3)),
+            pltpu.SemaphoreType.DMA((block_count, 4)),
+            pltpu.SemaphoreType.DMA((block_count, 4)),
+            pltpu.SemaphoreType.DMA,
             pltpu.SemaphoreType.DMA,
         ],
         compiler_params=pltpu.CompilerParams(
@@ -517,7 +546,7 @@
     return pl.pallas_call(
         functools.partial(smooth_kernel, (shots, rows, layers, span, cells)),
         out_shape=jax.ShapeDtypeStruct((layers, rows, cells), F32),
-        in_specs=[sm, vm],
+        in_specs=[sm, vm, vm],
         out_specs=vm,
         scratch_shapes=[
             pltpu.VMEM((cells // 128, rows * layers, 128), F32),
@@ -525,7 +554,7 @@
         ],
         compiler_params=pltpu.CompilerParams(vmem_limit_bytes=56 * 1024 * 1024),
         name="smooth",
-    )(footprint, received)
+    )(footprint, received, tails)
 
 
 def solution(mesh):

time: 144 us -> 125 us (0.87)
  Pallas kernels: 141 us -> 123 us
    pallas_call x1, Pallas kernels: 132 us -> 114 us  [on_device(): pl.pallas_call(functools.partial(wave_kernel, (rows, span, depth, block_c...]
where the time goes in v3:
time: 125 us
  Pallas kernels  123 us (98%)
  local copies, waits for them, and re-layouts  1.97 us (2%)
    pallas_call x1, Pallas kernels, on_device(): pl.pallas_call(functools.partial(wave_kernel, (rows, span, depth, block_c...  114 us
    pallas_call x1, Pallas kernels, on_device(): pl.pallas_call(functools.partial(smooth_kernel, (shots, rows, layers, spa...  9.07 us

profile of v3, /device:TPU:1, one launch (start us, length us, event | category | flops | bytes accessed | tf_op | source)
XLA Modules:
  0.0 125.1 jit_solution(684184170187236324)
XLA Ops:
  0.0 0.0 copy-start
  0.0 0.7 copy-done
  0.7 0.0 copy-start.1
  0.7 0.6 copy.20
  1.3 0.1 copy-done.1
  1.4 0.6 copy.19
  2.0 114.0 %wave.1 = (bf16[4,16,32,256]{3,2,1,0:T(8,128)(2,1)}, bf16[4,32,128]{2,1,0:T(8,128)(2,1)}) custom-call(s32[1,3]{1,0:T(1,128)} %source_pos.1, f32[1,3]{1,0:T(1,128)} %wavelet.1, s32[4,4]{1,0:T(4,128)} %footprint.3, s32[4]{0:T(128)} %owner.1, bf16[4096,128]{1,0:T(8,128)(2,1)} %bitcast.12, bf16[4096,128]{1,0:T(8,128)(2,1)} %bitcast.13, ...), custom_call_target="tpu_custom_call" | custom-call | tf_op jit(solution)/shard_map/wave/pallas_call | solution.py:500
  116.0 9.1 %smooth.1 = f32[32,16,256]{2,1,0:T(8,128)} custom-call(s32[4,4]{1,0:T(4,128)} %footprint.3, bf16[4,16,32,256]{3,2,1,0:T(8,128)(2,1)} %get-tuple-element.7.images, bf16[4,32,128]{2,1,0:T(8,128)(2,1)} %get-tuple-element.8.tails), custom_call_target="tpu_custom_call" | custom-call | tf_op jit(solution)/shard_map/smooth/pallas_call | solution.py:546
Async XLA Ops:
  0.0 0.7 copy-start
  0.7 0.7 copy-start.1
